TPU v7x, 32 devices: a whole 2x2x4 slice. The times are simulated.
32 devices in a mesh: field: 2 (over core), tm: 16 (over z, y, x).
Axes of the slice: x: 2, y: 2, z: 4, core: 2. Of those that a mesh axis runs over, the one named last changes fastest.
Arguments:
- observed: float32 [2, 262144], P('field', 'tm'), may hold values from -6 to 6
- weights: float32 [2, 262144], P('field', 'tm'), may hold values from 0.5 to 4
- features: float32 [2, 8, 262144], P('field', None, 'tm'), may hold values from -4 to 4
- source_ids: int32 [2, 262144], P('field', 'tm'), may hold values from 0 to 8191
- ccd_ids: int32 [2, 262144], P('field', 'tm'), may hold values from 0 to 61
- unit_ids: int32 [2, 262144], P('field', 'tm'), may hold values from 0 to 3
- counts: int32 [2, 512], P('field', 'tm'), may hold values from 256 to 512, as said below
- shared_cal: float32 [64, 4, 62], P('tm'), may hold values from -3 to 3
- field_cal: float32 [2, 64, 4, 62], P('field', 'tm'), may hold values from -3 to 3
Outputs:
- source_mean: float32 [262144], P(('field', 'tm'))
- new_shared: float32 [2, 64, 4, 62], P('field', 'tm')
- new_field: float32 [2, 64, 4, 62], P('field', 'tm')
Inputs may be any that keep to these rules, and one draw needn't show every extreme that they name: `counts`: every device sends at most 512 live transits to each owner; one owner receives exactly 512 from every device; live transits fill the first slots of a block.
All inputs are finite; a program needn't handle non-finite values.
Results may differ from a plain program's by a relative error of at most 0.0003.
Values sent between devices are 32-bit elements; how exact they have to be, the bound alone decides.
A program may use at most 64 MiB of HBM per device.

v0:
```python
import functools

import jax
import jax.numpy as jnp
from jax import lax
from jax.experimental import pallas as pl
from jax.experimental.pallas import tpu as pltpu
from jax.sharding import PartitionSpec as P

SRC_DEV = 8192
RIDGE = 1.0
UNROLL = 8
LANES = 128
SUB = 8
F32 = jnp.float32
BF16 = jnp.bfloat16
CCD_PAD = 64


def split_pair(x):
    high = x.astype(BF16).astype(F32)
    return jnp.concatenate([x, x - high], axis=0).astype(BF16)


def row_of(x, j, rows):
    return jnp.broadcast_to(x[j : j + 1, :], (rows, x.shape[1]))


def bf16_rows(count):
    return lax.broadcasted_iota(jnp.int32, (count, LANES), 0).astype(F32).astype(BF16)


def wide_row(row, count):
    one = jnp.broadcast_to(row.astype(F32), (2 * SUB, LANES)).astype(BF16)
    return jnp.concatenate([one] * (count // (2 * SUB)), axis=0)


def hot_rows(index_row, rows):
    hit = rows == wide_row(index_row, rows.shape[0])
    return jnp.where(hit, jnp.ones_like(rows), jnp.zeros_like(rows))


def pick(table, index):
    return jnp.take_along_axis(table, index, axis=1, mode="promise_in_bounds")


def nt_dot(left, right):
    return lax.dot_general(
        left, right, (((1,), (1,)), ((), ())), preferred_element_type=F32
    )


def build_tables(shared_ref, field_ref, tab_ref):
    units, n_shared, ccds = shared_ref.shape
    tab_ref[...] = jnp.zeros_like(tab_ref)
    for u in range(units):
        tab_ref[u, 0:n_shared, 0:ccds] = shared_ref[u]
        tab_ref[u, n_shared : 2 * n_shared, 0:ccds] = field_ref[u]


def used_weights(g, wts, cnt_ref, rows_per_block):
    sub = lax.broadcasted_iota(jnp.int32, (SUB, LANES), 0)
    lane = lax.broadcasted_iota(jnp.int32, (SUB, LANES), 1)
    position = (sub % rows_per_block) * LANES + lane
    per_group = SUB // rows_per_block
    limit = jnp.full((SUB, LANES), cnt_ref[0, g * per_group], jnp.int32)
    for b in range(1, per_group):
        limit = jnp.where(sub >= b * rows_per_block, cnt_ref[0, g * per_group + b], limit)
    return jnp.where(position < limit, wts, 0.0)


def feat_rows(feat_ref, row):
    return feat_ref[:, pl.ds(pl.multiple_of(row * LANES, LANES), LANES)]


def calibrate_rows(g, obs, ccd, unit, feat_ref, tables):
    index = ccd + (unit & 1) * CCD_PAD
    corrections = []
    for j in range(SUB):
        index_b = row_of(index, j, SUB)
        unit_b = row_of(unit, j, SUB)
        picked = jnp.where(unit_b < 2, pick(tables[0], index_b), pick(tables[1], index_b))
        corrections.append(jnp.sum(feat_rows(feat_ref, g * SUB + j) * picked, axis=0, keepdims=True))
    return obs - jnp.concatenate(corrections, axis=0)


def masked_units(pairs, unit_row, units):
    unit_b = jnp.broadcast_to(unit_row.astype(F32), (2 * SUB, LANES)).astype(BF16)
    zero = jnp.zeros((2 * SUB, LANES), BF16)
    out = []
    for u in range(units):
        own = unit_b == jnp.asarray(u, BF16)
        out += [jnp.where(own, pair, zero) for pair in pairs]
    return jnp.concatenate(out, axis=0)


def matrix_rows(g, weight_used, ccd, unit, feat_ref, units, ccd_rows):
    sub = lax.broadcasted_iota(jnp.int32, (SUB, LANES), 0) % 4
    left, hot = [], []
    for j in range(SUB):
        feats = feat_rows(feat_ref, g * SUB + j)
        weighted = row_of(weight_used, j, SUB) * feats
        next_one = jnp.where(sub == 3, pltpu.roll(feats, 3, 0), pltpu.roll(feats, 7, 0))
        next_two = jnp.where(sub >= 2, pltpu.roll(feats, 2, 0), pltpu.roll(feats, 6, 0))
        pairs = [split_pair(weighted * other) for other in (feats, next_one, next_two)]
        left.append(masked_units(pairs, unit[j : j + 1, :], units))
        hot.append(hot_rows(ccd[j : j + 1, :], ccd_rows))
    return nt_dot(jnp.concatenate(left, axis=1), jnp.concatenate(hot, axis=1))


def vector_rows(g, scaled, ccd, unit, feat_ref, units, ccd_rows):
    left, hot = [], []
    for j in range(SUB):
        feats = feat_rows(feat_ref, g * SUB + j)
        left.append(masked_units([split_pair(row_of(scaled, j, SUB) * feats)], unit[j : j + 1, :], units))
        hot.append(hot_rows(ccd[j : j + 1, :], ccd_rows))
    return nt_dot(jnp.concatenate(left, axis=1), jnp.concatenate(hot, axis=1))


def source_rows(values, ids, high_rows, low_rows):
    high, low = ids >> 7, ids & (LANES - 1)
    top = values.astype(BF16).astype(F32)
    rest = values - top
    zero = jnp.zeros_like(high_rows)
    count = high_rows.shape[0]
    left, hot = [], []
    for j in range(SUB):
        hot.append(hot_rows(low[j : j + 1, :], low_rows))
        hit = high_rows == wide_row(high[j : j + 1, :], count)
        left.append(jnp.concatenate(
            [jnp.where(hit, wide_row(x[j : j + 1, :], count), zero) for x in (top, rest)], axis=0))
    return nt_dot(jnp.concatenate(left, axis=1), jnp.concatenate(hot, axis=1))


def read_rows(mean_ref, ids):
    high, low = ids >> 7, ids & (LANES - 1)
    out = jnp.zeros((SUB, LANES), F32)
    for h in range(SRC_DEV // LANES):
        row = jnp.broadcast_to(mean_ref[h : h + 1, :], (SUB, LANES))
        out = jnp.where(high == h, pick(row, low), out)
    return out


def solve_rows(matrix, vector):
    n = len(vector)
    a = [[None] * n for _ in range(n)]
    for i in range(n):
        a[i][i] = matrix[0][i] + RIDGE
        k = (i + 1) % n
        a[i][k] = a[k][i] = matrix[1][i]
    for i in range(n // 2):
        a[i][i + 2] = a[i + 2][i] = matrix[2][i]
    b = list(vector)
    for p in range(n):
        for i in range(p + 1, n):
            factor = a[i][p] / a[p][p]
            for j in range(p, n):
                a[i][j] = a[i][j] - factor * a[p][j]
            b[i] = b[i] - factor * b[p]
    x = [None] * n
    for i in reversed(range(n)):
        running = b[i]
        for j in range(i + 1, n):
            running = running - a[i][j] * x[j]
        x[i] = running / a[i][i]
    return x


def whole_kernel(
    n_tm, rows_per_block,
    obs_h, wts_h, src_h, ccd_h, unit_h, feat_h, cnt_h, shared_h, field_h,
    mean_ref, new_shared_ref, new_field_ref,
    obs_ref, wts_ref, src_ref, ccd_ref, unit_ref, feat_ref, cnt_ref, shared_ref, field_ref,
    tab_ref, wu_ref, cal_ref, pack, pack_in, vals, vals_in, ans, ans_in,
    mat_ref, vec_ref, val_sum, wt_sum, mx, mx_in, vx, vx_in,
    load_sem, send_sem, recv_sem,
):
    units, n, ccds = shared_ref.shape
    devices = pack.shape[0]
    groups = obs_ref.shape[0] // SUB
    field, tm = lax.axis_index("field"), lax.axis_index("tm")
    me = field * n_tm + tm
    my_group = me // (SUB // rows_per_block)

    loads = [
        pltpu.make_async_copy(a, b, load_sem.at[i])
        for i, (a, b) in enumerate((
            (wts_h, wts_ref), (src_h, src_ref), (cnt_h, cnt_ref), (shared_h, shared_ref), (field_h, field_ref),
            (obs_h, obs_ref), (ccd_h, ccd_ref), (unit_h, unit_ref), (feat_h, feat_ref)))
    ]
    for load in loads:
        load.start()

    def wrap(x, size):
        return jnp.where(x >= size, x - size, x)

    def place(e):
        return jnp.where(e >= n_tm, 1, 0), wrap(e, n_tm)

    def target(k):
        e = wrap(me + k, devices)
        return e, place(e)

    barrier = pltpu.get_barrier_semaphore()

    def greet(k, carry):
        pl.semaphore_signal(barrier, inc=1, device_id=target(k)[1], device_id_type=pl.DeviceIdType.MESH)
        return carry

    for k in range(1, devices):
        greet(k, 0)

    def send(phase, source, landing, e):
        pltpu.make_async_remote_copy(
            src_ref=source.at[e], dst_ref=landing.at[me], send_sem=send_sem.at[phase], recv_sem=recv_sem.at[phase],
            device_id=place(e), device_id_type=pl.DeviceIdType.MESH).start()

    def await_bytes(ref, sem):
        part = ref.at[pl.ds(0, devices - 1)]
        pltpu.make_async_copy(part, part, sem).wait()

    def rows_at(g):
        return pl.ds(pl.multiple_of(g * SUB, SUB), SUB)

    def pair(ref, g):
        per = SUB // rows_per_block
        return jnp.concatenate([ref[g * per + b, 0:rows_per_block, :] for b in range(per)], axis=0)

    def weights_in(g):
        per = SUB // rows_per_block
        return jnp.concatenate([pack_in[g * per + b, rows_per_block:, :] for b in range(per)], axis=0)

    def ids_in(g):
        return pair(pack_in, g).astype(jnp.int32)

    def put(ref, g, x, first=0):
        per = SUB // rows_per_block
        for b in range(per):
            ref[g * per + b, first : first + rows_per_block, :] = x[b * rows_per_block : (b + 1) * rows_per_block]

    def turn(step):
        return wrap(my_group + step, groups)

    def in_halves(body, phase, source, landing):
        per = SUB // rows_per_block
        base = my_group * per
        half = groups // 2
        for part in range(2):
            lax.fori_loop(part * half, (part + 1) * half, body, 0, unroll=UNROLL)
            if part == 0:
                for i in range(1, per):
                    send(phase, source, landing, base + lax.rem(me - base + i, per))
            for k in range(part * half * per + (per if part == 0 else 0), (part + 1) * half * per):
                send(phase, source, landing, wrap(base + k, devices))

    for load in loads[:3]:
        load.wait()

    def prepare(g, carry):
        wu = used_weights(g, wts_ref[rows_at(g), :], cnt_ref, rows_per_block)
        wu_ref[rows_at(g), :] = wu
        put(pack, g, src_ref[rows_at(g), :].astype(F32))
        put(pack, g, wu, rows_per_block)
        return carry

    lax.fori_loop(0, groups, prepare, 0, unroll=UNROLL)
    pack_in[me] = pack[me]
    pl.semaphore_wait(barrier, devices - 1)

    def send_pack(k, carry):
        send(0, pack, pack_in, target(k)[0])
        return carry

    for k in range(1, devices):
        send_pack(k, 0)

    for load in loads[3:]:
        load.wait()
    build_tables(shared_ref, field_ref, tab_ref)
    tables = [tab_ref[2 * t] + pltpu.roll(tab_ref[2 * t + 1], CCD_PAD, 1) for t in range(units // 2)]

    def calibrate(step, carry):
        g = turn(step)
        at = rows_at(g)
        cal = calibrate_rows(g, obs_ref[at, :], ccd_ref[at, :], unit_ref[at, :], feat_ref, tables)
        cal_ref[at, :] = cal
        put(vals, g, wu_ref[at, :] * cal)
        return carry

    in_halves(calibrate, 1, vals, vals_in)
    vals_in[me] = vals[me]

    ccd_rows, low_rows = bf16_rows(CCD_PAD), bf16_rows(LANES)
    high_rows = bf16_rows(SRC_DEV // LANES)
    mat_ref[...] = jnp.zeros_like(mat_ref)
    vec_ref[...] = jnp.zeros_like(vec_ref)
    val_sum[...] = jnp.zeros_like(val_sum)
    wt_sum[...] = jnp.zeros_like(wt_sum)

    def add_matrix(g, carry):
        at = rows_at(g)
        mat_ref[...] += matrix_rows(g, wu_ref[at, :], ccd_ref[at, :], unit_ref[at, :], feat_ref, units, ccd_rows)
        return carry

    lax.fori_loop(0, groups, add_matrix, 0, unroll=UNROLL)

    def entry(ref, pieces, piece, row):
        out = []
        for u in range(units):
            base = (u * pieces + piece) * 2 * SUB + row
            out.append(ref[base : base + 1, :] + ref[base + SUB : base + SUB + 1, :])
        return jnp.concatenate(out, axis=0)

    def partner_copy(source, landing, phase):
        return pltpu.make_async_remote_copy(
            src_ref=source, dst_ref=landing, send_sem=send_sem.at[phase], recv_sem=recv_sem.at[phase],
            device_id=(1 - field, tm), device_id_type=pl.DeviceIdType.MESH)

    for d in range(3):
        for i in range(n):
            mx[d * n + i] = entry(mat_ref, 3, d, i)
    matrix_copy = partner_copy(mx, mx_in, 3)
    matrix_copy.start()

    await_bytes(pack_in, recv_sem.at[0])

    def add_weights(g, carry):
        wt_sum[...] += source_rows(weights_in(g), ids_in(g), high_rows, low_rows)
        return carry

    lax.fori_loop(0, groups, add_weights, 0, unroll=UNROLL)
    await_bytes(vals_in, recv_sem.at[1])

    def add_values(g, carry):
        val_sum[...] += source_rows(pair(vals_in, g), ids_in(g), high_rows, low_rows)
        return carry

    lax.fori_loop(0, groups, add_values, 0, unroll=UNROLL)
    count = SRC_DEV // LANES
    mean_ref[...] = (val_sum[:count] + val_sum[count:]) / ((wt_sum[:count] + wt_sum[count:]) + 1.0)

    def answer(step, carry):
        g = turn(step)
        put(ans, g, read_rows(mean_ref, ids_in(g)))
        return carry

    in_halves(answer, 2, ans, ans_in)
    ans_in[me] = ans[me]
    await_bytes(ans_in, recv_sem.at[2])

    def add_vector(g, carry):
        at = rows_at(g)
        scaled = wu_ref[at, :] * (cal_ref[at, :] - pair(ans_in, g))
        vec_ref[...] += vector_rows(g, scaled, ccd_ref[at, :], unit_ref[at, :], feat_ref, units, ccd_rows)
        return carry

    lax.fori_loop(0, groups, add_vector, 0, unroll=UNROLL)
    for i in range(n):
        vx[i] = entry(vec_ref, 1, 0, i)
    vector_copy = partner_copy(vx, vx_in, 4)
    vector_copy.start()

    def finish(matrix, vector, old_ref, new_ref):
        for i, x in enumerate(solve_rows(matrix, vector)):
            for u in range(units):
                new_ref[u, i : i + 1, :] = old_ref[u, i : i + 1, :] + x[u : u + 1, :ccds]

    finish([[entry(mat_ref, 3, d, n + i) for i in range(n)] for d in range(3)],
           [entry(vec_ref, 1, 0, n + i) for i in range(n)], field_ref, new_field_ref)
    matrix_copy.wait()
    vector_copy.wait()
    finish([[mx[d * n + i] + mx_in[d * n + i] for i in range(n)] for d in range(3)],
           [vx[i] + vx_in[i] for i in range(n)], shared_ref, new_shared_ref)
    await_bytes(pack, send_sem.at[0])
    await_bytes(vals, send_sem.at[1])
    await_bytes(ans, send_sem.at[2])


def per_device(n_tm, observed, weights, features, source_ids, ccd_ids, unit_ids, counts, shared_cal, field_cal):
    slots = observed.shape[1]
    devices = counts.shape[1]
    rows = slots // LANES
    block = rows // devices
    units, n, ccds = shared_cal.shape
    obs, wts, src, ccd, unit = (
        x.reshape(rows, LANES) for x in (observed, weights, source_ids, ccd_ids, unit_ids))
    high = SRC_DEV // LANES
    vm = lambda *shape: pltpu.VMEM(shape, F32)
    vi = lambda *shape: pltpu.VMEM(shape, jnp.int32)
    blocks = vm(devices, block, LANES)
    mean, new_shared, new_field = pl.pallas_call(
        functools.partial(whole_kernel, n_tm, block),
        out_shape=[
            jax.ShapeDtypeStruct((high, LANES), F32),
            jax.ShapeDtypeStruct((units, n, ccds), F32),
            jax.ShapeDtypeStruct((units, n, ccds), F32),
        ],
        in_specs=[pl.BlockSpec(memory_space=pl.ANY)] * 9,
        out_specs=[pl.BlockSpec(memory_space=pltpu.VMEM)] * 3,
        scratch_shapes=[
            vm(rows, LANES), vm(rows, LANES), vi(rows, LANES), vi(rows, LANES), vi(rows, LANES),
            vm(2 * n, slots), pltpu.SMEM((1, devices), jnp.int32), vm(units, n, ccds), vm(units, n, ccds),
            vm(units, 2 * n, LANES), vm(rows, LANES), vm(rows, LANES),
            vm(devices, 2 * block, LANES), vm(devices, 2 * block, LANES), blocks, blocks, blocks, blocks,
            vm(units * 3 * 2 * SUB, CCD_PAD), vm(units * 2 * SUB, CCD_PAD), vm(2 * high, LANES), vm(2 * high, LANES),
            vm(3 * n, units, CCD_PAD), vm(3 * n, units, CCD_PAD), vm(n, units, CCD_PAD), vm(n, units, CCD_PAD),
            pltpu.SemaphoreType.DMA((9,)), pltpu.SemaphoreType.DMA((5,)), pltpu.SemaphoreType.DMA((5,)),
        ],
        compiler_params=pltpu.CompilerParams(
            collective_id=0, has_side_effects=True, vmem_limit_bytes=56 * 1024 * 1024),
    )(obs, wts, src, ccd, unit, features[0], counts, shared_cal, field_cal[0])
    return mean.reshape(SRC_DEV), new_shared[None], new_field[None]


def solution(mesh):
    in_specs = (
        P("field", "tm"),
        P("field", "tm"),
        P("field", None, "tm"),
        P("field", "tm"),
        P("field", "tm"),
        P("field", "tm"),
        P("field", "tm"),
        P("tm", None, None),
        P("field", "tm", None, None),
    )
    out_specs = (P(("field", "tm")), P("field", "tm", None, None), P("field", "tm", None, None))
    return jax.shard_map(
        functools.partial(per_device, mesh.shape["tm"]), mesh=mesh, in_specs=in_specs, out_specs=out_specs, check_vma=False
    )
```

profile of v0, /device:TPU:0, one launch (start us, length us, event | category | flops | bytes accessed | tf_op | source)
XLA Modules:
  0.0 27.1 jit_solution(14253556332160636907)
XLA Ops:
  0.6 23.8 %shard_map.112 = (f32[64,128]{1,0:T(8,128)}, f32[4,4,62]{2,1,0:T(4,128)}, f32[4,4,62]{2,1,0:T(4,128)}) custom-call(f32[128,128]{1,0:T(8,128)} %bitcast.11, f32[128,128]{1,0:T(8,128)} %bitcast.12, s32[128,128]{1,0:T(8,128)} %bitcast.13, s32[128,128]{1,0:T(8,128)} %bitcast.14, s32[128,128]{1,0:T(8,128)} %bitcast.15, f32[8,16384]{1,0:T(8,128)} %bitcast.10, ...), custom_call_target="tpu_custom_call" | custom-call | tf_op jit(solution)/shard_map/pallas_call | solution.py:391
  24.4 0.0 copy-start.1
  24.4 1.4 %copy.15 = f32[8192]{0:T(1024)} copy(f32[8192]{0:T(1024)} %bitcast.16) | data formatting | bytes 65536
  25.8 0.0 copy-done.1
  25.8 0.0 copy-start
  25.8 0.6 %copy.16 = f32[1,4,4,62]{3,2,1,0:T(4,128)} copy(f32[1,4,4,62]{3,2,1,0:T(4,128)S(1)} %bitcast.19) | data formatting | bytes 7936
  26.4 0.1 copy-done
  26.5 0.6 %copy.17 = f32[1,4,4,62]{3,2,1,0:T(4,128)} copy(f32[1,4,4,62]{3,2,1,0:T(4,128)S(1)} %bitcast.18) | data formatting | bytes 7936
Async XLA Ops:
  24.4 1.4 %copy-start.1 = (f32[4,4,62]{2,1,0:T(4,128)S(1)}, f32[4,4,62]{2,1,0:T(4,128)}, u32[]{:S(2)}) copy-start(f32[4,4,62]{2,1,0:T(4,128)} %get-tuple-element.7) | copy-start | bytes 11908
  25.8 0.7 %copy-start = (f32[4,4,62]{2,1,0:T(4,128)S(1)}, f32[4,4,62]{2,1,0:T(4,128)}, u32[]{:S(2)}) copy-start(f32[4,4,62]{2,1,0:T(4,128)} %get-tuple-element.8) | copy-start | bytes 11908
where the time goes:
time: 27.4 us; the launch traced here: 27.1 us
  Pallas kernels  23.8 us (87%)
  local copies, waits for them, and re-layouts  2.68 us (10%)
  between operations  0.65 us (2%)
    pallas_call x1, Pallas kernels, per_device(): pl.pallas_call(functools.partial(whole_kernel, n_tm, block), out_shape=[j...  23.8 us
    unnamed x7, local copies, waits for them, and re-layouts  2.68 us

commit v1 on v0

--- a/solution.py
+++ b/solution.py
@@ -376,6 +376,14 @@
     await_bytes(ans, send_sem.at[2])
 
 
+def hand_on(*refs):
+    copies = [pltpu.make_async_copy(refs[i], refs[3 + i], refs[6].at[i]) for i in range(3)]
+    for copy in copies:
+        copy.start()
+    for copy in copies:
+        copy.wait()
+
+
 def per_device(n_tm, observed, weights, features, source_ids, ccd_ids, unit_ids, counts, shared_cal, field_cal):
     slots = observed.shape[1]
     devices = counts.shape[1]
@@ -390,11 +398,7 @@
     blocks = vm(devices, block, LANES)
     mean, new_shared, new_field = pl.pallas_call(
         functools.partial(whole_kernel, n_tm, block),
-        out_shape=[
-            jax.ShapeDtypeStruct((high, LANES), F32),
-            jax.ShapeDtypeStruct((units, n, ccds), F32),
-            jax.ShapeDtypeStruct((units, n, ccds), F32),
-        ],
+        out_shape=[pltpu.VMEM((high, LANES), F32), pltpu.VMEM((units, n, ccds), F32), pltpu.VMEM((units, n, ccds), F32)],
         in_specs=[pl.BlockSpec(memory_space=pl.ANY)] * 9,
         out_specs=[pl.BlockSpec(memory_space=pltpu.VMEM)] * 3,
         scratch_shapes=[
@@ -409,6 +413,13 @@
         compiler_params=pltpu.CompilerParams(
             collective_id=0, has_side_effects=True, vmem_limit_bytes=56 * 1024 * 1024),
     )(obs, wts, src, ccd, unit, features[0], counts, shared_cal, field_cal[0])
+    mean, new_shared, new_field = pl.pallas_call(
+        hand_on,
+        out_shape=[jax.ShapeDtypeStruct(x.shape, F32) for x in (mean, new_shared, new_field)],
+        in_specs=[pl.BlockSpec(memory_space=pl.ANY)] * 3,
+        out_specs=[pl.BlockSpec(memory_space=pl.ANY)] * 3,
+        scratch_shapes=[pltpu.SemaphoreType.DMA((3,))],
+    )(*(pltpu.with_memory_space_constraint(x, pltpu.VMEM) for x in (mean, new_shared, new_field)))
     return mean.reshape(SRC_DEV), new_shared[None], new_field[None]
 
 

time: 27.4 us -> 24.6 us (0.90)
  local copies, waits for them, and re-layouts: 2.68 us -> 0 us
    unnamed x7 -> x0, local copies, waits for them, and re-layouts: 2.68 us -> none
    pallas_call x1 -> x2, Pallas kernels: 23.8 us -> 23.8 us  [the longest x1 23.2 us: per_device(): pl.pallas_call(functools.partial(whole_kernel, n_tm, block), out_shape=[p...]
where the time goes in v1:
time: 24.6 us; the launch traced here: 24.5 us
  Pallas kernels  23.8 us (97%)
  between operations  0.64 us (3%)
    pallas_call x1, Pallas kernels, per_device(): pl.pallas_call(functools.partial(whole_kernel, n_tm, block), out_shape=[p...  23.2 us
    pallas_call x1, Pallas kernels, per_device(): pl.pallas_call(hand_on, out_shape=[jax.ShapeDtypeStruct(x.shape, F32) for...  0.65 us

profile of v1, /device:TPU:0, one launch (start us, length us, event | category | flops | bytes accessed | tf_op | source)
XLA Modules:
  0.0 24.5 jit_solution(5572806208944094872)
XLA Ops:
  0.6 23.2 %shard_map.112 = (f32[64,128]{1,0:T(8,128)S(1)}, f32[4,4,62]{2,1,0:T(4,128)S(1)}, f32[4,4,62]{2,1,0:T(4,128)S(1)}) custom-call(f32[128,128]{1,0:T(8,128)} %bitcast.11, f32[128,128]{1,0:T(8,128)} %bitcast.12, s32[128,128]{1,0:T(8,128)} %bitcast.13, s32[128,128]{1,0:T(8,128)} %bitcast.14, s32[128,128]{1,0:T(8,128)} %bitcast.15, f32[8,16384]{1,0:T(8,128)} %bitcast.10, ...), custom_call_target="tpu_custom_call" | custom-call | tf_op jit(solution)/shard_map/pallas_call | solution.py:399
  23.8 0.6 %shard_map.113 = (f32[64,128]{1,0:T(8,128)}, f32[4,4,62]{2,1,0:T(4,128)}, f32[4,4,62]{2,1,0:T(4,128)}) custom-call(f32[64,128]{1,0:T(8,128)S(1)} %get-tuple-element.9.refs_0_, f32[4,4,62]{2,1,0:T(4,128)S(1)} %get-tuple-element.10.refs_1_, f32[4,4,62]{2,1,0:T(4,128)S(1)} %get-tuple-element.11.refs_2_), custom_call_target="tpu_custom_call" | custom-call | tf_op jit(solution)/shard_map/pallas_call | solution.py:416

commit v2 on v1

--- a/solution.py
+++ b/solution.py
@@ -10,6 +10,8 @@
 SRC_DEV = 8192
 RIDGE = 1.0
 UNROLL = 8
+CHUNK = 4
+CHUNK_UNROLL = 4
 LANES = 128
 SUB = 8
 F32 = jnp.float32
@@ -117,10 +119,12 @@
     return nt_dot(jnp.concatenate(left, axis=1), jnp.concatenate(hot, axis=1))
 
 
-def source_rows(values, ids, high_rows, low_rows):
+def source_rows(ids, weights, values, high_rows, low_rows):
     high, low = ids >> 7, ids & (LANES - 1)
-    top = values.astype(BF16).astype(F32)
-    rest = values - top
+    pieces = []
+    for x in (weights, values):
+        top = x.astype(BF16).astype(F32)
+        pieces += [top, x - top]
     zero = jnp.zeros_like(high_rows)
     count = high_rows.shape[0]
     left, hot = [], []
@@ -128,7 +132,7 @@
         hot.append(hot_rows(low[j : j + 1, :], low_rows))
         hit = high_rows == wide_row(high[j : j + 1, :], count)
         left.append(jnp.concatenate(
-            [jnp.where(hit, wide_row(x[j : j + 1, :], count), zero) for x in (top, rest)], axis=0))
+            [jnp.where(hit, wide_row(x[j : j + 1, :], count), zero) for x in pieces], axis=0))
     return nt_dot(jnp.concatenate(left, axis=1), jnp.concatenate(hot, axis=1))
 
 
@@ -171,16 +175,32 @@
     obs_h, wts_h, src_h, ccd_h, unit_h, feat_h, cnt_h, shared_h, field_h,
     mean_ref, new_shared_ref, new_field_ref,
     obs_ref, wts_ref, src_ref, ccd_ref, unit_ref, feat_ref, cnt_ref, shared_ref, field_ref,
-    tab_ref, wu_ref, cal_ref, pack, pack_in, vals, vals_in, ans, ans_in,
-    mat_ref, vec_ref, val_sum, wt_sum, mx, mx_in, vx, vx_in,
-    load_sem, send_sem, recv_sem,
+    tab_ref, wu_ref, cal_ref, pack, pack_in, ans, ans_in,
+    mat_ref, vec_ref, sum_ref, mx, mx_in, vx, vx_in,
+    load_sem, send_sem, recv_sem, chunk_sem,
 ):
     units, n, ccds = shared_ref.shape
     devices = pack.shape[0]
     groups = obs_ref.shape[0] // SUB
+    per = SUB // rows_per_block
+    chunk = CHUNK * per
+    chunks = devices // chunk
+    ring = chunks // 2
     field, tm = lax.axis_index("field"), lax.axis_index("tm")
     me = field * n_tm + tm
-    my_group = me // (SUB // rows_per_block)
+    my_chunk = me // chunk
+    my_part = my_chunk % ring
+
+    def wrap(x, size):
+        return jnp.where(x >= size, x - size, x)
+
+    def place(e):
+        return jnp.where(e >= n_tm, 1, 0), wrap(e, n_tm)
+
+    barrier = pltpu.get_barrier_semaphore()
+    for k in range(1, devices):
+        pl.semaphore_signal(
+            barrier, inc=1, device_id=place(wrap(me + k, devices)), device_id_type=pl.DeviceIdType.MESH)
 
     loads = [
         pltpu.make_async_copy(a, b, load_sem.at[i])
@@ -191,111 +211,72 @@
     for load in loads:
         load.start()
 
-    def wrap(x, size):
-        return jnp.where(x >= size, x - size, x)
-
-    def place(e):
-        return jnp.where(e >= n_tm, 1, 0), wrap(e, n_tm)
-
-    def target(k):
-        e = wrap(me + k, devices)
-        return e, place(e)
-
-    barrier = pltpu.get_barrier_semaphore()
-
-    def greet(k, carry):
-        pl.semaphore_signal(barrier, inc=1, device_id=target(k)[1], device_id_type=pl.DeviceIdType.MESH)
-        return carry
-
-    for k in range(1, devices):
-        greet(k, 0)
-
-    def send(phase, source, landing, e):
-        pltpu.make_async_remote_copy(
-            src_ref=source.at[e], dst_ref=landing.at[me], send_sem=send_sem.at[phase], recv_sem=recv_sem.at[phase],
-            device_id=place(e), device_id_type=pl.DeviceIdType.MESH).start()
-
-    def await_bytes(ref, sem):
+    def chunk_near(step):
+        turn, other = step // 2, step % 2
+        ahead = jnp.where(turn % 2 == 1, (turn + 1) // 2, wrap(ring - turn // 2, ring))
+        return wrap(field + other, 2) * ring + wrap(my_part + ahead, ring)
+
+    def send_chunk(phase, source, landing, c, first=0):
+        for i in range(first, chunk):
+            e = c * chunk + (me + i) % chunk
+            pltpu.make_async_remote_copy(
+                src_ref=source.at[e], dst_ref=landing.at[me], send_sem=send_sem.at[phase],
+                recv_sem=chunk_sem.at[phase, my_chunk], device_id=place(e), device_id_type=pl.DeviceIdType.MESH).start()
+        if first:
+            pltpu.make_async_copy(source.at[me], landing.at[me], chunk_sem.at[phase, my_chunk]).start()
+
+    def await_chunk(phase, landing, c):
+        part = landing.at[pl.ds(c * chunk, chunk)]
+        pltpu.make_async_copy(part, part, chunk_sem.at[phase, c]).wait()
+
+    def await_sent(ref, sem):
         part = ref.at[pl.ds(0, devices - 1)]
         pltpu.make_async_copy(part, part, sem).wait()
 
     def rows_at(g):
         return pl.ds(pl.multiple_of(g * SUB, SUB), SUB)
 
-    def pair(ref, g):
-        per = SUB // rows_per_block
-        return jnp.concatenate([ref[g * per + b, 0:rows_per_block, :] for b in range(per)], axis=0)
-
-    def weights_in(g):
-        per = SUB // rows_per_block
-        return jnp.concatenate([pack_in[g * per + b, rows_per_block:, :] for b in range(per)], axis=0)
+    def pair(ref, g, k):
+        return jnp.concatenate([ref[g * per + b, k] for b in range(per)], axis=0)
 
     def ids_in(g):
-        return pair(pack_in, g).astype(jnp.int32)
-
-    def put(ref, g, x, first=0):
-        per = SUB // rows_per_block
+        return pair(pack_in, g, 0).astype(jnp.int32)
+
+    def put(ref, g, k, x):
         for b in range(per):
-            ref[g * per + b, first : first + rows_per_block, :] = x[b * rows_per_block : (b + 1) * rows_per_block]
-
-    def turn(step):
-        return wrap(my_group + step, groups)
-
-    def in_halves(body, phase, source, landing):
-        per = SUB // rows_per_block
-        base = my_group * per
-        half = groups // 2
-        for part in range(2):
-            lax.fori_loop(part * half, (part + 1) * half, body, 0, unroll=UNROLL)
-            if part == 0:
-                for i in range(1, per):
-                    send(phase, source, landing, base + lax.rem(me - base + i, per))
-            for k in range(part * half * per + (per if part == 0 else 0), (part + 1) * half * per):
-                send(phase, source, landing, wrap(base + k, devices))
-
-    for load in loads[:3]:
-        load.wait()
-
-    def prepare(g, carry):
-        wu = used_weights(g, wts_ref[rows_at(g), :], cnt_ref, rows_per_block)
-        wu_ref[rows_at(g), :] = wu
-        put(pack, g, src_ref[rows_at(g), :].astype(F32))
-        put(pack, g, wu, rows_per_block)
-        return carry
-
-    lax.fori_loop(0, groups, prepare, 0, unroll=UNROLL)
-    pack_in[me] = pack[me]
-    pl.semaphore_wait(barrier, devices - 1)
-
-    def send_pack(k, carry):
-        send(0, pack, pack_in, target(k)[0])
-        return carry
-
-    for k in range(1, devices):
-        send_pack(k, 0)
-
-    for load in loads[3:]:
+            ref[g * per + b, k] = x[b * rows_per_block : (b + 1) * rows_per_block]
+
+    for load in loads:
         load.wait()
     build_tables(shared_ref, field_ref, tab_ref)
     tables = [tab_ref[2 * t] + pltpu.roll(tab_ref[2 * t + 1], CCD_PAD, 1) for t in range(units // 2)]
 
-    def calibrate(step, carry):
-        g = turn(step)
+    def calibrate(g, carry):
         at = rows_at(g)
+        wu = used_weights(g, wts_ref[at, :], cnt_ref, rows_per_block)
         cal = calibrate_rows(g, obs_ref[at, :], ccd_ref[at, :], unit_ref[at, :], feat_ref, tables)
+        wu_ref[at, :] = wu
         cal_ref[at, :] = cal
-        put(vals, g, wu_ref[at, :] * cal)
-        return carry
-
-    in_halves(calibrate, 1, vals, vals_in)
-    vals_in[me] = vals[me]
+        put(pack, g, 0, src_ref[at, :].astype(F32))
+        put(pack, g, 1, wu)
+        put(pack, g, 2, wu * cal)
+        return carry
+
+    lax.fori_loop(0, groups, calibrate, 0, unroll=UNROLL)
+    pl.semaphore_wait(barrier, devices - 1)
+
+    def send_pack(step, carry):
+        send_chunk(0, pack, pack_in, chunk_near(1 + step))
+        return carry
+
+    send_chunk(0, pack, pack_in, my_chunk, 1)
+    lax.fori_loop(0, chunks - 1, send_pack, 0, unroll=CHUNK_UNROLL - 1)
 
     ccd_rows, low_rows = bf16_rows(CCD_PAD), bf16_rows(LANES)
     high_rows = bf16_rows(SRC_DEV // LANES)
     mat_ref[...] = jnp.zeros_like(mat_ref)
     vec_ref[...] = jnp.zeros_like(vec_ref)
-    val_sum[...] = jnp.zeros_like(val_sum)
-    wt_sum[...] = jnp.zeros_like(wt_sum)
+    sum_ref[...] = jnp.zeros_like(sum_ref)
 
     def add_matrix(g, carry):
         at = rows_at(g)
@@ -313,51 +294,66 @@
 
     def partner_copy(source, landing, phase):
         return pltpu.make_async_remote_copy(
-            src_ref=source, dst_ref=landing, send_sem=send_sem.at[phase], recv_sem=recv_sem.at[phase],
+            src_ref=source, dst_ref=landing, send_sem=send_sem.at[2 + phase], recv_sem=recv_sem.at[phase],
             device_id=(1 - field, tm), device_id_type=pl.DeviceIdType.MESH)
 
     for d in range(3):
         for i in range(n):
             mx[d * n + i] = entry(mat_ref, 3, d, i)
-    matrix_copy = partner_copy(mx, mx_in, 3)
+    matrix_copy = partner_copy(mx, mx_in, 0)
     matrix_copy.start()
 
-    await_bytes(pack_in, recv_sem.at[0])
-
-    def add_weights(g, carry):
-        wt_sum[...] += source_rows(weights_in(g), ids_in(g), high_rows, low_rows)
-        return carry
-
-    lax.fori_loop(0, groups, add_weights, 0, unroll=UNROLL)
-    await_bytes(vals_in, recv_sem.at[1])
-
-    def add_values(g, carry):
-        val_sum[...] += source_rows(pair(vals_in, g), ids_in(g), high_rows, low_rows)
-        return carry
-
-    lax.fori_loop(0, groups, add_values, 0, unroll=UNROLL)
+    def add_sources(step, carry):
+        both = [chunk_near(2 * step + k) for k in range(2)]
+        for c in both:
+            await_chunk(0, pack_in, c)
+        total = [sum_ref[k] for k in range(2)]
+        for b in range(2 * CHUNK):
+            g = both[b // CHUNK] * CHUNK + b % CHUNK
+            total[b % 2] += source_rows(ids_in(g), pair(pack_in, g, 1), pair(pack_in, g, 2), high_rows, low_rows)
+        for k in range(2):
+            sum_ref[k] = total[k]
+        return carry
+
+    lax.fori_loop(0, ring, add_sources, 0, unroll=2)
     count = SRC_DEV // LANES
-    mean_ref[...] = (val_sum[:count] + val_sum[count:]) / ((wt_sum[:count] + wt_sum[count:]) + 1.0)
+    sums = sum_ref[0] + sum_ref[1]
+    mean_ref[...] = (sums[2 * count : 3 * count] + sums[3 * count :]) / ((sums[:count] + sums[count : 2 * count]) + 1.0)
+
+    def answer_chunk(c):
+        for b in range(CHUNK):
+            g = c * CHUNK + b
+            put(ans, g, 0, read_rows(mean_ref, ids_in(g)))
 
     def answer(step, carry):
-        g = turn(step)
-        put(ans, g, read_rows(mean_ref, ids_in(g)))
-        return carry
-
-    in_halves(answer, 2, ans, ans_in)
-    ans_in[me] = ans[me]
-    await_bytes(ans_in, recv_sem.at[2])
-
-    def add_vector(g, carry):
-        at = rows_at(g)
-        scaled = wu_ref[at, :] * (cal_ref[at, :] - pair(ans_in, g))
-        vec_ref[...] += vector_rows(g, scaled, ccd_ref[at, :], unit_ref[at, :], feat_ref, units, ccd_rows)
-        return carry
-
-    lax.fori_loop(0, groups, add_vector, 0, unroll=UNROLL)
+        c = chunk_near(chunks - 1 - step)
+        answer_chunk(c)
+        send_chunk(1, ans, ans_in, c)
+        return carry
+
+    lax.fori_loop(0, chunks - 1, answer, 0, unroll=CHUNK_UNROLL - 1)
+    answer_chunk(my_chunk)
+    send_chunk(1, ans, ans_in, my_chunk, 1)
+
+    def add_vector(step, carry):
+        both = [chunk_near(2 * step + k) for k in range(2)]
+        for c in both:
+            await_chunk(1, ans_in, c)
+        total = [vec_ref[k] for k in range(2)]
+        for b in range(2 * CHUNK):
+            g = both[b // CHUNK] * CHUNK + b % CHUNK
+            at = rows_at(g)
+            scaled = wu_ref[at, :] * (cal_ref[at, :] - pair(ans_in, g, 0))
+            total[b % 2] += vector_rows(g, scaled, ccd_ref[at, :], unit_ref[at, :], feat_ref, units, ccd_rows)
+        for k in range(2):
+            vec_ref[k] = total[k]
+        return carry
+
+    lax.fori_loop(0, ring, add_vector, 0, unroll=2)
+    vec_ref[0] += vec_ref[1]
     for i in range(n):
-        vx[i] = entry(vec_ref, 1, 0, i)
-    vector_copy = partner_copy(vx, vx_in, 4)
+        vx[i] = entry(vec_ref.at[0], 1, 0, i)
+    vector_copy = partner_copy(vx, vx_in, 1)
     vector_copy.start()
 
     def finish(matrix, vector, old_ref, new_ref):
@@ -366,14 +362,13 @@
                 new_ref[u, i : i + 1, :] = old_ref[u, i : i + 1, :] + x[u : u + 1, :ccds]
 
     finish([[entry(mat_ref, 3, d, n + i) for i in range(n)] for d in range(3)],
-           [entry(vec_ref, 1, 0, n + i) for i in range(n)], field_ref, new_field_ref)
+           [entry(vec_ref.at[0], 1, 0, n + i) for i in range(n)], field_ref, new_field_ref)
+    await_sent(pack, send_sem.at[0])
+    await_sent(ans, send_sem.at[1])
     matrix_copy.wait()
     vector_copy.wait()
     finish([[mx[d * n + i] + mx_in[d * n + i] for i in range(n)] for d in range(3)],
            [vx[i] + vx_in[i] for i in range(n)], shared_ref, new_shared_ref)
-    await_bytes(pack, send_sem.at[0])
-    await_bytes(vals, send_sem.at[1])
-    await_bytes(ans, send_sem.at[2])
 
 
 def hand_on(*refs):
@@ -395,7 +390,8 @@
     high = SRC_DEV // LANES
     vm = lambda *shape: pltpu.VMEM(shape, F32)
     vi = lambda *shape: pltpu.VMEM(shape, jnp.int32)
-    blocks = vm(devices, block, LANES)
+    blocks = lambda kinds: vm(devices, kinds, block, LANES)
+    chunks = block * devices // (SUB * CHUNK)
     mean, new_shared, new_field = pl.pallas_call(
         functools.partial(whole_kernel, n_tm, block),
         out_shape=[pltpu.VMEM((high, LANES), F32), pltpu.VMEM((units, n, ccds), F32), pltpu.VMEM((units, n, ccds), F32)],
@@ -405,10 +401,11 @@
             vm(rows, LANES), vm(rows, LANES), vi(rows, LANES), vi(rows, LANES), vi(rows, LANES),
             vm(2 * n, slots), pltpu.SMEM((1, devices), jnp.int32), vm(units, n, ccds), vm(units, n, ccds),
             vm(units, 2 * n, LANES), vm(rows, LANES), vm(rows, LANES),
-            vm(devices, 2 * block, LANES), vm(devices, 2 * block, LANES), blocks, blocks, blocks, blocks,
-            vm(units * 3 * 2 * SUB, CCD_PAD), vm(units * 2 * SUB, CCD_PAD), vm(2 * high, LANES), vm(2 * high, LANES),
+            blocks(3), blocks(3), blocks(1), blocks(1),
+            vm(units * 3 * 2 * SUB, CCD_PAD), vm(2, units * 2 * SUB, CCD_PAD), vm(2, 4 * high, LANES),
             vm(3 * n, units, CCD_PAD), vm(3 * n, units, CCD_PAD), vm(n, units, CCD_PAD), vm(n, units, CCD_PAD),
-            pltpu.SemaphoreType.DMA((9,)), pltpu.SemaphoreType.DMA((5,)), pltpu.SemaphoreType.DMA((5,)),
+            pltpu.SemaphoreType.DMA((9,)), pltpu.SemaphoreType.DMA((4,)), pltpu.SemaphoreType.DMA((2,)),
+            pltpu.SemaphoreType.DMA((2, chunks)),
         ],
         compiler_params=pltpu.CompilerParams(
             collective_id=0, has_side_effects=True, vmem_limit_bytes=56 * 1024 * 1024),

time: 24.6 us -> 22.8 us (0.927)
  Pallas kernels: 23.8 us -> 22 us
    pallas_call x1, Pallas kernels: 23.2 us -> 21.4 us  [per_device(): pl.pallas_call(functools.partial(whole_kernel, n_tm, block), out_shape=[p...]
where the time goes in v2:
time: 22.8 us; the launch traced here: 22.7 us
  Pallas kernels  22 us (96%)
  between operations  0.64 us (3%)
    pallas_call x1, Pallas kernels, per_device(): pl.pallas_call(functools.partial(whole_kernel, n_tm, block), out_shape=[p...  21.4 us
    pallas_call x1, Pallas kernels, per_device(): pl.pallas_call(hand_on, out_shape=[jax.ShapeDtypeStruct(x.shape, F32) for...  0.65 us

profile of v2, /device:TPU:0, one launch (start us, length us, event | category | flops | bytes accessed | tf_op | source)
XLA Modules:
  0.0 22.7 jit_solution(12291363614784944529)
XLA Ops:
  0.6 21.4 %shard_map.112 = (f32[64,128]{1,0:T(8,128)S(1)}, f32[4,4,62]{2,1,0:T(4,128)S(1)}, f32[4,4,62]{2,1,0:T(4,128)S(1)}) custom-call(f32[128,128]{1,0:T(8,128)} %bitcast.11, f32[128,128]{1,0:T(8,128)} %bitcast.12, s32[128,128]{1,0:T(8,128)} %bitcast.13, s32[128,128]{1,0:T(8,128)} %bitcast.14, s32[128,128]{1,0:T(8,128)} %bitcast.15, f32[8,16384]{1,0:T(8,128)} %bitcast.10, ...), custom_call_target="tpu_custom_call" | custom-call | tf_op jit(solution)/shard_map/pallas_call | solution.py:395
  22.0 0.6 %shard_map.113 = (f32[64,128]{1,0:T(8,128)}, f32[4,4,62]{2,1,0:T(4,128)}, f32[4,4,62]{2,1,0:T(4,128)}) custom-call(f32[64,128]{1,0:T(8,128)S(1)} %get-tuple-element.9.refs_0_, f32[4,4,62]{2,1,0:T(4,128)S(1)} %get-tuple-element.10.refs_1_, f32[4,4,62]{2,1,0:T(4,128)S(1)} %get-tuple-element.11.refs_2_), custom_call_target="tpu_custom_call" | custom-call | tf_op jit(solution)/shard_map/pallas_call | solution.py:413

commit v3 on v2

--- a/solution.py
+++ b/solution.py
@@ -10,8 +10,10 @@
 SRC_DEV = 8192
 RIDGE = 1.0
 UNROLL = 8
-CHUNK = 4
-CHUNK_UNROLL = 4
+CHUNK = 2
+CHUNK_UNROLL = 8
+SPAN = 4
+WIDE = 2
 LANES = 128
 SUB = 8
 F32 = jnp.float32
@@ -145,8 +147,8 @@
     return out
 
 
-def solve_rows(matrix, vector):
-    n = len(vector)
+def factor_rows(matrix):
+    n = len(matrix[0])
     a = [[None] * n for _ in range(n)]
     for i in range(n):
         a[i][i] = matrix[0][i] + RIDGE
@@ -154,19 +156,29 @@
         a[i][k] = a[k][i] = matrix[1][i]
     for i in range(n // 2):
         a[i][i + 2] = a[i + 2][i] = matrix[2][i]
+    for p in range(n):
+        for i in range(p + 1, n):
+            factor = a[i][p] / a[p][p]
+            for j in range(p + 1, n):
+                a[i][j] = a[i][j] - factor * a[p][j]
+            a[i][p] = factor
+    for p in range(n):
+        a[p][p] = 1.0 / a[p][p]
+    return a
+
+
+def solve_rows(a, vector):
+    n = len(vector)
     b = list(vector)
     for p in range(n):
         for i in range(p + 1, n):
-            factor = a[i][p] / a[p][p]
-            for j in range(p, n):
-                a[i][j] = a[i][j] - factor * a[p][j]
-            b[i] = b[i] - factor * b[p]
+            b[i] = b[i] - a[i][p] * b[p]
     x = [None] * n
     for i in reversed(range(n)):
         running = b[i]
         for j in range(i + 1, n):
             running = running - a[i][j] * x[j]
-        x[i] = running / a[i][i]
+        x[i] = running * a[i][i]
     return x
 
 
@@ -176,7 +188,7 @@
     mean_ref, new_shared_ref, new_field_ref,
     obs_ref, wts_ref, src_ref, ccd_ref, unit_ref, feat_ref, cnt_ref, shared_ref, field_ref,
     tab_ref, wu_ref, cal_ref, pack, pack_in, ans, ans_in,
-    mat_ref, vec_ref, sum_ref, mx, mx_in, vx, vx_in,
+    mat_ref, vec_ref, sum_ref, mx, mx_in, vx, vx_in, lu_ref,
     load_sem, send_sem, recv_sem, chunk_sem,
 ):
     units, n, ccds = shared_ref.shape
@@ -198,9 +210,13 @@
         return jnp.where(e >= n_tm, 1, 0), wrap(e, n_tm)
 
     barrier = pltpu.get_barrier_semaphore()
-    for k in range(1, devices):
-        pl.semaphore_signal(
-            barrier, inc=1, device_id=place(wrap(me + k, devices)), device_id_type=pl.DeviceIdType.MESH)
+    bits = [1 << b for b in range(n_tm.bit_length() - 1)]
+    steps = [(1 - 2 * ((tm // bit) % 2)) * bit for bit in bits]
+    for k in reversed(range(n_tm)):
+        mate = tm + sum(step for bit, step in zip(bits, steps) if k & bit)
+        for other in range(2 if k else 1):
+            pl.semaphore_signal(
+                barrier, inc=1, device_id=(1 - field if other == 0 else field, mate), device_id_type=pl.DeviceIdType.MESH)
 
     loads = [
         pltpu.make_async_copy(a, b, load_sem.at[i])
@@ -211,10 +227,13 @@
     for load in loads:
         load.start()
 
+    def chunk_late(step):
+        return wrap(field + step % 2, 2) * ring + ring - 1 - step // 2
+
     def chunk_near(step):
         turn, other = step // 2, step % 2
-        ahead = jnp.where(turn % 2 == 1, (turn + 1) // 2, wrap(ring - turn // 2, ring))
-        return wrap(field + other, 2) * ring + wrap(my_part + ahead, ring)
+        part = sum((my_part // bit + turn // bit) % 2 * bit for bit in (1 << b for b in range(ring.bit_length() - 1)))
+        return wrap(field + other, 2) * ring + part
 
     def send_chunk(phase, source, landing, c, first=0):
         for i in range(first, chunk):
@@ -266,11 +285,17 @@
     pl.semaphore_wait(barrier, devices - 1)
 
     def send_pack(step, carry):
-        send_chunk(0, pack, pack_in, chunk_near(1 + step))
-        return carry
-
-    send_chunk(0, pack, pack_in, my_chunk, 1)
-    lax.fori_loop(0, chunks - 1, send_pack, 0, unroll=CHUNK_UNROLL - 1)
+        @pl.when(chunk_late(step) != my_chunk)
+        def _():
+            send_chunk(0, pack, pack_in, chunk_late(step))
+
+        @pl.when(chunk_late(step) == my_chunk)
+        def _():
+            send_chunk(0, pack, pack_in, my_chunk, 1)
+
+        return carry
+
+    lax.fori_loop(0, chunks, send_pack, 0, unroll=CHUNK_UNROLL)
 
     ccd_rows, low_rows = bf16_rows(CCD_PAD), bf16_rows(LANES)
     high_rows = bf16_rows(SRC_DEV // LANES)
@@ -304,18 +329,18 @@
     matrix_copy.start()
 
     def add_sources(step, carry):
-        both = [chunk_near(2 * step + k) for k in range(2)]
-        for c in both:
+        parts = [chunk_near(WIDE * step + k) for k in range(WIDE)]
+        for c in parts:
             await_chunk(0, pack_in, c)
         total = [sum_ref[k] for k in range(2)]
-        for b in range(2 * CHUNK):
-            g = both[b // CHUNK] * CHUNK + b % CHUNK
+        for b in range(WIDE * CHUNK):
+            g = parts[b // CHUNK] * CHUNK + b % CHUNK
             total[b % 2] += source_rows(ids_in(g), pair(pack_in, g, 1), pair(pack_in, g, 2), high_rows, low_rows)
         for k in range(2):
             sum_ref[k] = total[k]
         return carry
 
-    lax.fori_loop(0, ring, add_sources, 0, unroll=2)
+    lax.fori_loop(0, chunks // WIDE, add_sources, 0, unroll=4)
     count = SRC_DEV // LANES
     sums = sum_ref[0] + sum_ref[1]
     mean_ref[...] = (sums[2 * count : 3 * count] + sums[3 * count :]) / ((sums[:count] + sums[count : 2 * count]) + 1.0)
@@ -326,22 +351,38 @@
             put(ans, g, 0, read_rows(mean_ref, ids_in(g)))
 
     def answer(step, carry):
-        c = chunk_near(chunks - 1 - step)
+        c = chunk_late(chunks - 1 - step)
         answer_chunk(c)
-        send_chunk(1, ans, ans_in, c)
-        return carry
-
-    lax.fori_loop(0, chunks - 1, answer, 0, unroll=CHUNK_UNROLL - 1)
-    answer_chunk(my_chunk)
-    send_chunk(1, ans, ans_in, my_chunk, 1)
+
+        @pl.when(c != my_chunk)
+        def _():
+            send_chunk(1, ans, ans_in, c)
+
+        @pl.when(c == my_chunk)
+        def _():
+            send_chunk(1, ans, ans_in, my_chunk, 1)
+
+        return carry
+
+    lax.fori_loop(0, chunks, answer, 0, unroll=CHUNK_UNROLL)
+
+    def factor(which, matrix):
+        rows = factor_rows(matrix)
+        for i in range(n):
+            for j in range(n):
+                lu_ref[which, i * n + j] = rows[i][j]
+
+    factor(0, [[entry(mat_ref, 3, d, n + i) for i in range(n)] for d in range(3)])
+    matrix_copy.wait()
+    factor(1, [[mx[d * n + i] + mx_in[d * n + i] for i in range(n)] for d in range(3)])
 
     def add_vector(step, carry):
-        both = [chunk_near(2 * step + k) for k in range(2)]
-        for c in both:
+        parts = [chunk_near(SPAN * step + k) for k in range(SPAN)]
+        for c in parts:
             await_chunk(1, ans_in, c)
         total = [vec_ref[k] for k in range(2)]
-        for b in range(2 * CHUNK):
-            g = both[b // CHUNK] * CHUNK + b % CHUNK
+        for b in range(SPAN * CHUNK):
+            g = parts[b // CHUNK] * CHUNK + b % CHUNK
             at = rows_at(g)
             scaled = wu_ref[at, :] * (cal_ref[at, :] - pair(ans_in, g, 0))
             total[b % 2] += vector_rows(g, scaled, ccd_ref[at, :], unit_ref[at, :], feat_ref, units, ccd_rows)
@@ -349,26 +390,24 @@
             vec_ref[k] = total[k]
         return carry
 
-    lax.fori_loop(0, ring, add_vector, 0, unroll=2)
+    lax.fori_loop(0, chunks // SPAN, add_vector, 0, unroll=2)
     vec_ref[0] += vec_ref[1]
     for i in range(n):
         vx[i] = entry(vec_ref.at[0], 1, 0, i)
     vector_copy = partner_copy(vx, vx_in, 1)
     vector_copy.start()
 
-    def finish(matrix, vector, old_ref, new_ref):
-        for i, x in enumerate(solve_rows(matrix, vector)):
+    def finish(which, vector, old_ref, new_ref):
+        rows = [[lu_ref[which, i * n + j] for j in range(n)] for i in range(n)]
+        for i, x in enumerate(solve_rows(rows, vector)):
             for u in range(units):
                 new_ref[u, i : i + 1, :] = old_ref[u, i : i + 1, :] + x[u : u + 1, :ccds]
 
-    finish([[entry(mat_ref, 3, d, n + i) for i in range(n)] for d in range(3)],
-           [entry(vec_ref.at[0], 1, 0, n + i) for i in range(n)], field_ref, new_field_ref)
+    finish(0, [entry(vec_ref.at[0], 1, 0, n + i) for i in range(n)], field_ref, new_field_ref)
     await_sent(pack, send_sem.at[0])
     await_sent(ans, send_sem.at[1])
-    matrix_copy.wait()
     vector_copy.wait()
-    finish([[mx[d * n + i] + mx_in[d * n + i] for i in range(n)] for d in range(3)],
-           [vx[i] + vx_in[i] for i in range(n)], shared_ref, new_shared_ref)
+    finish(1, [vx[i] + vx_in[i] for i in range(n)], shared_ref, new_shared_ref)
 
 
 def hand_on(*refs):
@@ -404,6 +443,7 @@
             blocks(3), blocks(3), blocks(1), blocks(1),
             vm(units * 3 * 2 * SUB, CCD_PAD), vm(2, units * 2 * SUB, CCD_PAD), vm(2, 4 * high, LANES),
             vm(3 * n, units, CCD_PAD), vm(3 * n, units, CCD_PAD), vm(n, units, CCD_PAD), vm(n, units, CCD_PAD),
+            vm(2, n * n, units, CCD_PAD),
             pltpu.SemaphoreType.DMA((9,)), pltpu.SemaphoreType.DMA((4,)), pltpu.SemaphoreType.DMA((2,)),
             pltpu.SemaphoreType.DMA((2, chunks)),
         ],

time: 22.8 us -> 22.4 us (0.982)
  Pallas kernels: 22 us -> 21.6 us
    pallas_call x1, Pallas kernels: 21.4 us -> 20.9 us  [per_device(): pl.pallas_call(functools.partial(whole_kernel, n_tm, block), out_shape=[p...]
where the time goes in v3:
time: 22.4 us; the launch traced here: 22.2 us
  Pallas kernels  21.6 us (96%)
  between operations  0.64 us (3%)
    pallas_call x1, Pallas kernels, per_device(): pl.pallas_call(functools.partial(whole_kernel, n_tm, block), out_shape=[p...  20.9 us
    pallas_call x1, Pallas kernels, per_device(): pl.pallas_call(hand_on, out_shape=[jax.ShapeDtypeStruct(x.shape, F32) for...  0.65 us

profile of v3, /device:TPU:0, one launch (start us, length us, event | category | flops | bytes accessed | tf_op | source)
XLA Modules:
  0.0 22.2 jit_solution(12106098600869551379)
XLA Ops:
  0.6 20.9 %shard_map.112 = (f32[64,128]{1,0:T(8,128)S(1)}, f32[4,4,62]{2,1,0:T(4,128)S(1)}, f32[4,4,62]{2,1,0:T(4,128)S(1)}) custom-call(f32[128,128]{1,0:T(8,128)} %bitcast.11, f32[128,128]{1,0:T(8,128)} %bitcast.12, s32[128,128]{1,0:T(8,128)} %bitcast.13, s32[128,128]{1,0:T(8,128)} %bitcast.14, s32[128,128]{1,0:T(8,128)} %bitcast.15, f32[8,16384]{1,0:T(8,128)} %bitcast.10, ...), custom_call_target="tpu_custom_call" | custom-call | tf_op jit(solution)/shard_map/pallas_call | solution.py:434
  21.6 0.6 %shard_map.113 = (f32[64,128]{1,0:T(8,128)}, f32[4,4,62]{2,1,0:T(4,128)}, f32[4,4,62]{2,1,0:T(4,128)}) custom-call(f32[64,128]{1,0:T(8,128)S(1)} %get-tuple-element.9.refs_0_, f32[4,4,62]{2,1,0:T(4,128)S(1)} %get-tuple-element.10.refs_1_, f32[4,4,62]{2,1,0:T(4,128)S(1)} %get-tuple-element.11.refs_2_), custom_call_target="tpu_custom_call" | custom-call | tf_op jit(solution)/shard_map/pallas_call | solution.py:453

commit v4 on v3

--- a/solution.py
+++ b/solution.py
@@ -12,7 +12,7 @@
 UNROLL = 8
 CHUNK = 2
 CHUNK_UNROLL = 8
-SPAN = 4
+SPAN = 6
 WIDE = 2
 LANES = 128
 SUB = 8
@@ -244,6 +244,17 @@
         if first:
             pltpu.make_async_copy(source.at[me], landing.at[me], chunk_sem.at[phase, my_chunk]).start()
 
+    def send_other(phase, source, landing, e):
+        @pl.when(e != me)
+        def _():
+            pltpu.make_async_remote_copy(
+                src_ref=source.at[e], dst_ref=landing.at[me], send_sem=send_sem.at[phase],
+                recv_sem=chunk_sem.at[phase, my_chunk], device_id=place(e), device_id_type=pl.DeviceIdType.MESH).start()
+
+        @pl.when(e == me)
+        def _():
+            pltpu.make_async_copy(source.at[me], landing.at[me], chunk_sem.at[phase, my_chunk]).start()
+
     def await_chunk(phase, landing, c):
         part = landing.at[pl.ds(c * chunk, chunk)]
         pltpu.make_async_copy(part, part, chunk_sem.at[phase, c]).wait()
@@ -285,17 +296,13 @@
     pl.semaphore_wait(barrier, devices - 1)
 
     def send_pack(step, carry):
-        @pl.when(chunk_late(step) != my_chunk)
-        def _():
-            send_chunk(0, pack, pack_in, chunk_late(step))
-
-        @pl.when(chunk_late(step) == my_chunk)
-        def _():
-            send_chunk(0, pack, pack_in, my_chunk, 1)
-
-        return carry
-
-    lax.fori_loop(0, chunks, send_pack, 0, unroll=CHUNK_UNROLL)
+        part = ring - 1 - step
+        for i in reversed(range(chunk)):
+            for other in range(2):
+                send_other(0, pack, pack_in, (wrap(field + other, 2) * ring + part) * chunk + i)
+        return carry
+
+    lax.fori_loop(0, ring, send_pack, 0, unroll=CHUNK_UNROLL // 2)
 
     ccd_rows, low_rows = bf16_rows(CCD_PAD), bf16_rows(LANES)
     high_rows = bf16_rows(SRC_DEV // LANES)
@@ -345,26 +352,17 @@
     sums = sum_ref[0] + sum_ref[1]
     mean_ref[...] = (sums[2 * count : 3 * count] + sums[3 * count :]) / ((sums[:count] + sums[count : 2 * count]) + 1.0)
 
-    def answer_chunk(c):
+    def answer(part, carry):
         for b in range(CHUNK):
-            g = c * CHUNK + b
-            put(ans, g, 0, read_rows(mean_ref, ids_in(g)))
-
-    def answer(step, carry):
-        c = chunk_late(chunks - 1 - step)
-        answer_chunk(c)
-
-        @pl.when(c != my_chunk)
-        def _():
-            send_chunk(1, ans, ans_in, c)
-
-        @pl.when(c == my_chunk)
-        def _():
-            send_chunk(1, ans, ans_in, my_chunk, 1)
-
-        return carry
-
-    lax.fori_loop(0, chunks, answer, 0, unroll=CHUNK_UNROLL)
+            both = [(wrap(field + other, 2) * ring + part) * CHUNK + b for other in range(2)]
+            for g in both:
+                put(ans, g, 0, read_rows(mean_ref, ids_in(g)))
+            for g in both:
+                for k in range(per):
+                    send_other(1, ans, ans_in, g * per + k)
+        return carry
+
+    lax.fori_loop(0, ring, answer, 0, unroll=CHUNK_UNROLL // 2)
 
     def factor(which, matrix):
         rows = factor_rows(matrix)
@@ -376,21 +374,25 @@
     matrix_copy.wait()
     factor(1, [[mx[d * n + i] + mx_in[d * n + i] for i in range(n)] for d in range(3)])
 
-    def add_vector(step, carry):
-        parts = [chunk_near(SPAN * step + k) for k in range(SPAN)]
+    def add_vector(start, span):
+        parts = [chunk_near(start + k) for k in range(span)]
         for c in parts:
             await_chunk(1, ans_in, c)
         total = [vec_ref[k] for k in range(2)]
-        for b in range(SPAN * CHUNK):
+        for b in range(span * CHUNK):
             g = parts[b // CHUNK] * CHUNK + b % CHUNK
             at = rows_at(g)
             scaled = wu_ref[at, :] * (cal_ref[at, :] - pair(ans_in, g, 0))
             total[b % 2] += vector_rows(g, scaled, ccd_ref[at, :], unit_ref[at, :], feat_ref, units, ccd_rows)
         for k in range(2):
             vec_ref[k] = total[k]
-        return carry
-
-    lax.fori_loop(0, chunks // SPAN, add_vector, 0, unroll=2)
+
+    def add_early(step, carry):
+        add_vector(step * SPAN, SPAN)
+        return carry
+
+    lax.fori_loop(0, (chunks - 2) // SPAN, add_early, 0)
+    add_vector(chunks - 2, 2)
     vec_ref[0] += vec_ref[1]
     for i in range(n):
         vx[i] = entry(vec_ref.at[0], 1, 0, i)

time: 22.4 us -> 21.7 us (0.969)
  Pallas kernels: 21.6 us -> 20.9 us
    pallas_call x1, Pallas kernels: 20.9 us -> 20.3 us  [per_device(): pl.pallas_call(functools.partial(whole_kernel, n_tm, block), out_shape=[p...]
where the time goes in v4:
time: 21.7 us; the launch traced here: 21.6 us
  Pallas kernels  20.9 us (96%)
  between operations  0.64 us (3%)
    pallas_call x1, Pallas kernels, per_device(): pl.pallas_call(functools.partial(whole_kernel, n_tm, block), out_shape=[p...  20.3 us
    pallas_call x1, Pallas kernels, per_device(): pl.pallas_call(hand_on, out_shape=[jax.ShapeDtypeStruct(x.shape, F32) for...  0.65 us

profile of v4, /device:TPU:0, one launch (start us, length us, event | category | flops | bytes accessed | tf_op | source)
XLA Modules:
  0.0 21.6 jit_solution(9631990690123452877)
XLA Ops:
  0.6 20.3 %shard_map.112 = (f32[64,128]{1,0:T(8,128)S(1)}, f32[4,4,62]{2,1,0:T(4,128)S(1)}, f32[4,4,62]{2,1,0:T(4,128)S(1)}) custom-call(f32[128,128]{1,0:T(8,128)} %bitcast.11, f32[128,128]{1,0:T(8,128)} %bitcast.12, s32[128,128]{1,0:T(8,128)} %bitcast.13, s32[128,128]{1,0:T(8,128)} %bitcast.14, s32[128,128]{1,0:T(8,128)} %bitcast.15, f32[8,16384]{1,0:T(8,128)} %bitcast.10, ...), custom_call_target="tpu_custom_call" | custom-call | tf_op jit(solution)/shard_map/pallas_call | solution.py:436
  20.9 0.6 %shard_map.113 = (f32[64,128]{1,0:T(8,128)}, f32[4,4,62]{2,1,0:T(4,128)}, f32[4,4,62]{2,1,0:T(4,128)}) custom-call(f32[64,128]{1,0:T(8,128)S(1)} %get-tuple-element.9.refs_0_, f32[4,4,62]{2,1,0:T(4,128)S(1)} %get-tuple-element.10.refs_1_, f32[4,4,62]{2,1,0:T(4,128)S(1)} %get-tuple-element.11.refs_2_), custom_call_target="tpu_custom_call" | custom-call | tf_op jit(solution)/shard_map/pallas_call | solution.py:455

commit v5 on v4

--- a/solution.py
+++ b/solution.py
@@ -235,25 +235,27 @@
         part = sum((my_part // bit + turn // bit) % 2 * bit for bit in (1 << b for b in range(ring.bit_length() - 1)))
         return wrap(field + other, 2) * ring + part
 
-    def send_chunk(phase, source, landing, c, first=0):
-        for i in range(first, chunk):
-            e = c * chunk + (me + i) % chunk
-            pltpu.make_async_remote_copy(
-                src_ref=source.at[e], dst_ref=landing.at[me], send_sem=send_sem.at[phase],
-                recv_sem=chunk_sem.at[phase, my_chunk], device_id=place(e), device_id_type=pl.DeviceIdType.MESH).start()
-        if first:
-            pltpu.make_async_copy(source.at[me], landing.at[me], chunk_sem.at[phase, my_chunk]).start()
-
-    def send_other(phase, source, landing, e):
-        @pl.when(e != me)
+    def send(phase, source, landing, e):
+        pltpu.make_async_remote_copy(
+            src_ref=source.at[e], dst_ref=landing.at[me], send_sem=send_sem.at[phase],
+            recv_sem=chunk_sem.at[phase, my_chunk], device_id=place(e), device_id_type=pl.DeviceIdType.MESH).start()
+
+    def send_all(phase, source, landing, part, blocks):
+        @pl.when(part != my_part)
         def _():
-            pltpu.make_async_remote_copy(
-                src_ref=source.at[e], dst_ref=landing.at[me], send_sem=send_sem.at[phase],
-                recv_sem=chunk_sem.at[phase, my_chunk], device_id=place(e), device_id_type=pl.DeviceIdType.MESH).start()
-
-        @pl.when(e == me)
+            for e in blocks:
+                send(phase, source, landing, e)
+
+        @pl.when(part == my_part)
         def _():
-            pltpu.make_async_copy(source.at[me], landing.at[me], chunk_sem.at[phase, my_chunk]).start()
+            for e in blocks:
+                @pl.when(e != me)
+                def _():
+                    send(phase, source, landing, e)
+
+                @pl.when(e == me)
+                def _():
+                    pltpu.make_async_copy(source.at[me], landing.at[me], chunk_sem.at[phase, my_chunk]).start()
 
     def await_chunk(phase, landing, c):
         part = landing.at[pl.ds(c * chunk, chunk)]
@@ -297,9 +299,8 @@
 
     def send_pack(step, carry):
         part = ring - 1 - step
-        for i in reversed(range(chunk)):
-            for other in range(2):
-                send_other(0, pack, pack_in, (wrap(field + other, 2) * ring + part) * chunk + i)
+        sides = [(wrap(field + other, 2) * ring + part) * chunk for other in range(2)]
+        send_all(0, pack, pack_in, part, [side + i for i in reversed(range(chunk)) for side in sides])
         return carry
 
     lax.fori_loop(0, ring, send_pack, 0, unroll=CHUNK_UNROLL // 2)
@@ -357,9 +358,7 @@
             both = [(wrap(field + other, 2) * ring + part) * CHUNK + b for other in range(2)]
             for g in both:
                 put(ans, g, 0, read_rows(mean_ref, ids_in(g)))
-            for g in both:
-                for k in range(per):
-                    send_other(1, ans, ans_in, g * per + k)
+            send_all(1, ans, ans_in, part, [g * per + k for k in range(per) for g in both])
         return carry
 
     lax.fori_loop(0, ring, answer, 0, unroll=CHUNK_UNROLL // 2)

time: 21.7 us -> 21.7 us (level)
  no operation moved by 1% of the time
where the time goes in v5:
time: 21.7 us; the launch traced here: 21.6 us
  Pallas kernels  21 us (97%)
  between operations  0.64 us (3%)
    pallas_call x1, Pallas kernels, per_device(): pl.pallas_call(functools.partial(whole_kernel, n_tm, block), out_shape=[p...  20.3 us
    pallas_call x1, Pallas kernels, per_device(): pl.pallas_call(hand_on, out_shape=[jax.ShapeDtypeStruct(x.shape, F32) for...  0.65 us

profile of v5, /device:TPU:0, one launch (start us, length us, event | category | flops | bytes accessed | tf_op | source)
XLA Modules:
  0.0 21.6 jit_solution(3762440831647508138)
XLA Ops:
  0.6 20.3 %shard_map.112 = (f32[64,128]{1,0:T(8,128)S(1)}, f32[4,4,62]{2,1,0:T(4,128)S(1)}, f32[4,4,62]{2,1,0:T(4,128)S(1)}) custom-call(f32[128,128]{1,0:T(8,128)} %bitcast.11, f32[128,128]{1,0:T(8,128)} %bitcast.12, s32[128,128]{1,0:T(8,128)} %bitcast.13, s32[128,128]{1,0:T(8,128)} %bitcast.14, s32[128,128]{1,0:T(8,128)} %bitcast.15, f32[8,16384]{1,0:T(8,128)} %bitcast.10, ...), custom_call_target="tpu_custom_call" | custom-call | tf_op jit(solution)/shard_map/pallas_call | solution.py:435
  20.9 0.6 %shard_map.113 = (f32[64,128]{1,0:T(8,128)}, f32[4,4,62]{2,1,0:T(4,128)}, f32[4,4,62]{2,1,0:T(4,128)}) custom-call(f32[64,128]{1,0:T(8,128)S(1)} %get-tuple-element.9.refs_0_, f32[4,4,62]{2,1,0:T(4,128)S(1)} %get-tuple-element.10.refs_1_, f32[4,4,62]{2,1,0:T(4,128)S(1)} %get-tuple-element.11.refs_2_), custom_call_target="tpu_custom_call" | custom-call | tf_op jit(solution)/shard_map/pallas_call | solution.py:454

commit v6 on v5

--- a/solution.py
+++ b/solution.py
@@ -355,10 +355,10 @@
 
     def answer(part, carry):
         for b in range(CHUNK):
-            both = [(wrap(field + other, 2) * ring + part) * CHUNK + b for other in range(2)]
-            for g in both:
+            for other in range(2):
+                g = (wrap(field + other, 2) * ring + part) * CHUNK + b
                 put(ans, g, 0, read_rows(mean_ref, ids_in(g)))
-            send_all(1, ans, ans_in, part, [g * per + k for k in range(per) for g in both])
+                send_all(1, ans, ans_in, part, [g * per + k for k in range(per)])
         return carry
 
     lax.fori_loop(0, ring, answer, 0, unroll=CHUNK_UNROLL // 2)

time: 21.7 us -> 21.7 us (level)
  no operation moved by 1% of the time
where the time goes in v6:
time: 21.7 us; the launch traced here: 21.5 us
  Pallas kernels  20.9 us (96%)
  between operations  0.64 us (3%)
    pallas_call x1, Pallas kernels, per_device(): pl.pallas_call(functools.partial(whole_kernel, n_tm, block), out_shape=[p...  20.2 us
    pallas_call x1, Pallas kernels, per_device(): pl.pallas_call(hand_on, out_shape=[jax.ShapeDtypeStruct(x.shape, F32) for...  0.65 us

profile of v6, /device:TPU:0, one launch (start us, length us, event | category | flops | bytes accessed | tf_op | source)
XLA Modules:
  0.0 21.5 jit_solution(3369687776748067628)
XLA Ops:
  0.6 20.2 %shard_map.112 = (f32[64,128]{1,0:T(8,128)S(1)}, f32[4,4,62]{2,1,0:T(4,128)S(1)}, f32[4,4,62]{2,1,0:T(4,128)S(1)}) custom-call(f32[128,128]{1,0:T(8,128)} %bitcast.11, f32[128,128]{1,0:T(8,128)} %bitcast.12, s32[128,128]{1,0:T(8,128)} %bitcast.13, s32[128,128]{1,0:T(8,128)} %bitcast.14, s32[128,128]{1,0:T(8,128)} %bitcast.15, f32[8,16384]{1,0:T(8,128)} %bitcast.10, ...), custom_call_target="tpu_custom_call" | custom-call | tf_op jit(solution)/shard_map/pallas_call | solution.py:435
  20.9 0.6 %shard_map.113 = (f32[64,128]{1,0:T(8,128)}, f32[4,4,62]{2,1,0:T(4,128)}, f32[4,4,62]{2,1,0:T(4,128)}) custom-call(f32[64,128]{1,0:T(8,128)S(1)} %get-tuple-element.9.refs_0_, f32[4,4,62]{2,1,0:T(4,128)S(1)} %get-tuple-element.10.refs_1_, f32[4,4,62]{2,1,0:T(4,128)S(1)} %get-tuple-element.11.refs_2_), custom_call_target="tpu_custom_call" | custom-call | tf_op jit(solution)/shard_map/pallas_call | solution.py:454
